TPU v7x, 32 devices: a whole 2x2x4 slice. The times are simulated.
32 devices in a mesh: rows: 8 (over y, x, core), heads: 4 (over z).
Axes of the slice: x: 2, y: 2, z: 4, core: 2. Of those that a mesh axis runs over, the one named last changes fastest.
Arguments:
- layer_in: bfloat16 [32768, 768], P(('rows', 'heads')), may hold values from -6 to 6
- segment_ids: int32 [64, 512], P('rows'), may hold values from 0 to 3, never falling along the last dimension, each value on 1 to 256 neighbouring positions
- w_query: bfloat16 [768, 768], P(None, 'heads'), may hold values from -0.21875 to 0.21875
- w_key: bfloat16 [768, 768], P(None, 'heads'), may hold values from -0.21875 to 0.21875
- w_value: bfloat16 [768, 768], P(None, 'heads'), may hold values from -0.21875 to 0.21875
- b_query: bfloat16 [768], P('heads'), may hold values from -3 to 3
- b_value: bfloat16 [768], P('heads'), may hold values from -3 to 3
- w_output: bfloat16 [768, 768], replicated, may hold values from -0.875 to 0.875
- b_output: float32 [768], replicated, may hold values from -3 to 3
- gain_attn: float32 [768], replicated, may hold values from 0.5 to 1.5
- shift_attn: float32 [768], replicated, may hold values from -3 to 3
- w_inner: bfloat16 [768, 3072], replicated, may hold values from -0.21875 to 0.21875
- b_inner: float32 [3072], replicated, may hold values from -3 to 3
- w_outer: bfloat16 [3072, 768], replicated, may hold values from -0.109375 to 0.109375
- b_outer: float32 [768], replicated, may hold values from -3 to 3
- gain_ffn: float32 [768], replicated, may hold values from 0.5 to 1.5
- shift_ffn: float32 [768], replicated, may hold values from -3 to 3
- cotangent: bfloat16 [32768, 768], P(('rows', 'heads')), may hold values from -6 to 6
Outputs:
- layer_out: bfloat16 [32768, 768], P(('rows', 'heads'))
- input_grad: float32 [32768, 768], P(('rows', 'heads'))
- w_query_grad: float32 [768, 768], P(None, 'heads')
- w_key_grad: float32 [768, 768], P(None, 'heads')
- w_value_grad: float32 [768, 768], P(None, 'heads')
- b_query_grad: float32 [768], P('heads')
- b_value_grad: float32 [768], P('heads')
- w_output_grad: float32 [768, 768], replicated
- b_output_grad: float32 [768], replicated
- gain_attn_grad: float32 [768], replicated
- shift_attn_grad: float32 [768], replicated
- w_inner_grad: float32 [768, 3072], P(None, ('rows', 'heads'))
- b_inner_grad: float32 [3072], P(('rows', 'heads'))
- w_outer_grad: float32 [3072, 768], P(('rows', 'heads'))
- b_outer_grad: float32 [768], replicated
- gain_ffn_grad: float32 [768], replicated
- shift_ffn_grad: float32 [768], replicated
Inputs may be any that keep to these rules, and one draw needn't show every extreme that they name: `segment_ids`: within each packed row the ids number its documents in order, never falling; every row holds 256 positions of one document at most, and some document reaches that.
All inputs are finite; a program needn't handle non-finite values.
Results may differ from a plain program's by a relative error of at most 0.015.
Values may be sent and summed in bfloat16 or wider, within the bound.
No kernel may reach another device: no remote copies, remote signals or barrier semaphores. Data moves between devices by JAX's collectives and lax.ppermute only.
A program may use at most 192 MiB of HBM per device.

v0:
```python
import jax
import jax.numpy as jnp
from jax import lax
from jax.sharding import PartitionSpec as P

HD = 64


epsilon = 1e-06
masked_score = -1000000000.0


def gelu_value(values):
    return 0.5 * values * (1.0 + lax.erf(values * 0.7071067811865476))


def gelu_slope(values):
    cumulative = 0.5 * (1.0 + lax.erf(values * 0.7071067811865476))
    density = jnp.exp(-0.5 * values * values) * 0.3989422804014327
    return cumulative + values * density


def norm_forward(values, gain_row, shift_row):
    mean_value = jnp.mean(values, -1, keepdims=True)
    centred = values - mean_value
    variance = jnp.mean(centred * centred, -1, keepdims=True)
    rstd_rows = lax.rsqrt(variance + epsilon)
    normal = centred * rstd_rows
    return (normal * gain_row + shift_row, normal, rstd_rows)


def norm_backward(grad_rows, normal, rstd_rows, gain_row):
    scaled = grad_rows * gain_row
    return rstd_rows * (
        scaled
        - jnp.mean(scaled, -1, keepdims=True)
        - normal * jnp.mean(scaled * normal, -1, keepdims=True)
    )


def masked_scores(query_seq, keys_seq, seg_seq, scaling):
    scores = (
        jnp.einsum("qhc,khc->hqk", query_seq, keys_seq, preferred_element_type=jnp.float32)
        * scaling
    )
    same_doc = seg_seq[:, None] == seg_seq[None, :]
    return jnp.where(same_doc[None], scores, masked_score)


def attend_forward(query, keys_all, values_all, segments, scaling):
    count_seq, length = segments.shape
    heads_here = query.shape[1] // HD

    def one_sequence(sequence_parts):
        query_seq, keys_seq, values_seq, seg_seq = sequence_parts
        query_seq = query_seq.reshape(length, heads_here, HD)
        keys_seq = keys_seq.reshape(length, heads_here, HD)
        values_seq = values_seq.reshape(length, heads_here, HD)
        scores = masked_scores(query_seq, keys_seq, seg_seq, scaling)
        highest = jnp.max(scores, -1, keepdims=True)
        exponent = jnp.exp(scores - highest)
        totals = jnp.sum(exponent, -1, keepdims=True)
        weights_low = (exponent / totals).astype(jnp.bfloat16)
        context = jnp.einsum(
            "hqk,khc->qhc", weights_low, values_seq, preferred_element_type=jnp.float32
        )
        return (
            context.reshape(length, heads_here * HD).astype(jnp.bfloat16),
            highest + jnp.log(totals),
        )

    context, log_sums = lax.map(
        one_sequence,
        (
            query.reshape(count_seq, length, -1),
            keys_all.reshape(count_seq, length, -1),
            values_all.reshape(count_seq, length, -1),
            segments,
        ),
    )
    return (context.reshape(count_seq * length, -1), log_sums)


def attend_backward(query, keys_all, values_all, segments, log_sums, grad_context, scaling):
    count_seq, length = segments.shape
    heads_here = query.shape[1] // HD

    def one_sequence(sequence_parts):
        query_seq, keys_seq, values_seq, seg_seq, log_seq, grad_seq = sequence_parts
        query_seq = query_seq.reshape(length, heads_here, HD)
        keys_seq = keys_seq.reshape(length, heads_here, HD)
        values_seq = values_seq.reshape(length, heads_here, HD)
        grad_seq = grad_seq.reshape(length, heads_here, HD)
        scores = masked_scores(query_seq, keys_seq, seg_seq, scaling)
        probs_full = jnp.exp(scores - log_seq)
        grad_probs = jnp.einsum(
            "qhc,khc->hqk", grad_seq, values_seq, preferred_element_type=jnp.float32
        )
        grad_values = jnp.einsum(
            "hqk,qhc->khc",
            probs_full.astype(jnp.bfloat16),
            grad_seq,
            preferred_element_type=jnp.float32,
        )
        inner_sum = jnp.sum(probs_full * grad_probs, -1, keepdims=True)
        grad_scores = (probs_full * (grad_probs - inner_sum)).astype(jnp.bfloat16)
        grad_query = (
            jnp.einsum("hqk,khc->qhc", grad_scores, keys_seq, preferred_element_type=jnp.float32)
            * scaling
        )
        grad_keys = (
            jnp.einsum("hqk,qhc->khc", grad_scores, query_seq, preferred_element_type=jnp.float32)
            * scaling
        )
        flat_shape = (length, heads_here * HD)
        return (
            grad_query.reshape(flat_shape).astype(jnp.bfloat16),
            grad_keys.reshape(flat_shape).astype(jnp.bfloat16),
            grad_values.reshape(flat_shape).astype(jnp.bfloat16),
        )

    grad_query, grad_keys, grad_values = lax.map(
        one_sequence,
        (
            query.reshape(count_seq, length, -1),
            keys_all.reshape(count_seq, length, -1),
            values_all.reshape(count_seq, length, -1),
            segments,
            log_sums,
            grad_context.reshape(count_seq, length, -1),
        ),
    )
    rows_all = count_seq * length
    return (
        grad_query.reshape(rows_all, -1),
        grad_keys.reshape(rows_all, -1),
        grad_values.reshape(rows_all, -1),
    )


def project_tokens(layer_in, query_full, key_full, value_full, bias_query, bias_value):
    query_tok = (
        jnp.dot(layer_in, query_full, preferred_element_type=jnp.float32) + bias_query
    ).astype(jnp.bfloat16)
    keys_tok = jnp.dot(layer_in, key_full, preferred_element_type=jnp.float32).astype(jnp.bfloat16)
    values_tok = (
        jnp.dot(layer_in, value_full, preferred_element_type=jnp.float32) + bias_value
    ).astype(jnp.bfloat16)
    return (query_tok, keys_tok, values_tok)


def local(
    layer_in,
    segment_ids,
    w_query,
    w_key,
    w_value,
    b_query,
    b_value,
    w_output,
    b_output,
    gain_attn,
    shift_attn,
    w_inner,
    b_inner,
    w_outer,
    b_outer,
    gain_ffn,
    shift_ffn,
    cotangent,
):
    scaling = HD ** (-0.5)
    gathered = lax.all_gather(layer_in, "heads", axis=0, tiled=True)
    query, keys_all, values_all = project_tokens(
        gathered, w_query, w_key, w_value, b_query, b_value
    )
    context, log_sums = attend_forward(query, keys_all, values_all, segment_ids, scaling)
    context_tok = lax.all_to_all(context, "heads", split_axis=0, concat_axis=1, tiled=True)
    inputs_wide = layer_in.astype(jnp.float32)
    branch = jnp.dot(context_tok, w_output, preferred_element_type=jnp.float32) + b_output
    normed, normal_one, rstd_one = norm_forward(inputs_wide + branch, gain_attn, shift_attn)
    normed_low = normed.astype(jnp.bfloat16)
    inner_pre = jnp.dot(normed_low, w_inner, preferred_element_type=jnp.float32) + b_inner
    active = gelu_value(inner_pre).astype(jnp.bfloat16)
    outer_out = jnp.dot(active, w_outer, preferred_element_type=jnp.float32) + b_outer
    result, normal_two, rstd_two = norm_forward(normed + outer_out, gain_ffn, shift_ffn)
    layer_out = result.astype(jnp.bfloat16)
    grad_result = cotangent.astype(jnp.float32)
    grad_gain_ffn = jnp.sum(grad_result * normal_two, 0)
    grad_shift_ffn = jnp.sum(grad_result, 0)
    grad_sum_two = norm_backward(grad_result, normal_two, rstd_two, gain_ffn)
    grad_outer = grad_sum_two.astype(jnp.bfloat16)
    grad_b_outer = jnp.sum(grad_outer.astype(jnp.float32), 0)
    grad_w_outer = jnp.einsum("ti,td->id", active, grad_outer, preferred_element_type=jnp.float32)
    grad_active = jnp.einsum("td,id->ti", grad_outer, w_outer, preferred_element_type=jnp.float32)
    grad_inner = (grad_active * gelu_slope(inner_pre)).astype(jnp.bfloat16)
    grad_w_inner = jnp.einsum(
        "td,ti->di", normed_low, grad_inner, preferred_element_type=jnp.float32
    )
    grad_b_inner = jnp.sum(grad_inner.astype(jnp.float32), 0)
    grad_normed = grad_sum_two + jnp.einsum(
        "ti,di->td", grad_inner, w_inner, preferred_element_type=jnp.float32
    )
    grad_gain_attn = jnp.sum(grad_normed * normal_one, 0)
    grad_shift_attn = jnp.sum(grad_normed, 0)
    grad_sum_one = norm_backward(grad_normed, normal_one, rstd_one, gain_attn)
    grad_branch = grad_sum_one.astype(jnp.bfloat16)
    grad_b_output = jnp.sum(grad_branch.astype(jnp.float32), 0)
    grad_w_output = jnp.einsum(
        "tc,td->cd", context_tok, grad_branch, preferred_element_type=jnp.float32
    )
    grad_context_tok = jnp.einsum(
        "td,cd->tc", grad_branch, w_output, preferred_element_type=jnp.float32
    ).astype(jnp.bfloat16)
    grad_context = lax.all_to_all(
        grad_context_tok, "heads", split_axis=1, concat_axis=0, tiled=True
    )
    grad_query, grad_keys, grad_values = attend_backward(
        query, keys_all, values_all, segment_ids, log_sums, grad_context, scaling
    )
    grad_heads_in = lax.psum_scatter(
        (
            jnp.einsum("tc,dc->td", grad_query, w_query, preferred_element_type=jnp.float32)
            + jnp.einsum("tc,dc->td", grad_keys, w_key, preferred_element_type=jnp.float32)
            + jnp.einsum("tc,dc->td", grad_values, w_value, preferred_element_type=jnp.float32)
        ).astype(jnp.bfloat16),
        "heads",
        scatter_dimension=0,
        tiled=True,
    ).astype(jnp.float32)
    grad_w_query = jnp.einsum("td,tc->dc", gathered, grad_query, preferred_element_type=jnp.float32)
    grad_w_key = jnp.einsum("td,tc->dc", gathered, grad_keys, preferred_element_type=jnp.float32)
    grad_w_value = jnp.einsum(
        "td,tc->dc", gathered, grad_values, preferred_element_type=jnp.float32
    )
    grad_b_query = jnp.sum(grad_query.astype(jnp.float32), 0)
    grad_b_value = jnp.sum(grad_values.astype(jnp.float32), 0)
    grad_w_query, grad_w_key, grad_w_value, grad_b_query, grad_b_value = lax.psum(
        (grad_w_query, grad_w_key, grad_w_value, grad_b_query, grad_b_value), "rows"
    )
    (
        grad_w_output,
        grad_b_output,
        grad_gain_attn,
        grad_shift_attn,
        grad_b_outer,
        grad_gain_ffn,
        grad_shift_ffn,
    ) = lax.psum(
        (
            grad_w_output,
            grad_b_output,
            grad_gain_attn,
            grad_shift_attn,
            grad_b_outer,
            grad_gain_ffn,
            grad_shift_ffn,
        ),
        ("rows", "heads"),
    )
    grad_w_inner, grad_w_outer, grad_b_inner = (
        lax.psum_scatter(grad_w_inner, ("rows", "heads"), scatter_dimension=1, tiled=True),
        lax.psum_scatter(grad_w_outer, ("rows", "heads"), scatter_dimension=0, tiled=True),
        lax.psum_scatter(grad_b_inner, ("rows", "heads"), scatter_dimension=0, tiled=True),
    )
    input_grad = grad_sum_one + grad_heads_in
    return (
        layer_out,
        input_grad,
        grad_w_query,
        grad_w_key,
        grad_w_value,
        grad_b_query,
        grad_b_value,
        grad_w_output,
        grad_b_output,
        grad_gain_attn,
        grad_shift_attn,
        grad_w_inner,
        grad_b_inner,
        grad_w_outer,
        grad_b_outer,
        grad_gain_ffn,
        grad_shift_ffn,
    )


def solution(mesh):
    return jax.shard_map(
        local,
        mesh=mesh,
        in_specs=(
            P(("rows", "heads"), None),
            P("rows", None),
            P(None, "heads"),
            P(None, "heads"),
            P(None, "heads"),
            P("heads"),
            P("heads"),
            P(),
            P(),
            P(),
            P(),
            P(),
            P(),
            P(),
            P(),
            P(),
            P(),
            P(("rows", "heads"), None),
        ),
        out_specs=(
            P(("rows", "heads"), None),
            P(("rows", "heads"), None),
            P(None, "heads"),
            P(None, "heads"),
            P(None, "heads"),
            P("heads"),
            P("heads"),
            P(),
            P(),
            P(),
            P(),
            P(None, ("rows", "heads")),
            P(("rows", "heads")),
            P(("rows", "heads"), None),
            P(),
            P(),
            P(),
        ),
        check_vma=False,
    )
```

profile of v0, /device:TPU:0, one launch (start us, length us, event | category | flops | bytes accessed | tf_op | source)
XLA Modules:
  0.0 1059.3 jit_solution(13024470438508607962)
XLA Ops:
  9.3 118.4 %all-gather.2.cloned.1.call-done = bf16[4096,768]{1,0:T(8,128)(2,1)} async-done(((bf16[1024,768]{1,0:T(8,128)(2,1)}), bf16[4096,768]{1,0:T(8,128)(2,1)}) %all-gather.2.cloned.1.call-update) | async-done | bytes 6291472 | tf_op jit(solution)/shard_map/all_gather | solution.py:173
  127.7 5.1 fusion.19
  133.8 2.2 convolution_convert_fusion
  136.0 2.2 fusion.20
  138.2 1.9 copy_bitcast_fusion
  141.4 42.5 %while.26 = (s32[]{:T(128)}, bf16[8,512,192]{1,2,0:T(8,128)(2,1)}, f32[8,3,512,1]{2,1,3,0:T(4,128)S(1)}, bf16[8,512,192]{1,2,0:T(8,128)(2,1)S(1)}, s32[8,512]{1,...) while((s32[]{:T(128)}, bf16[8,512,192]{1,2,0:T(8,128)(2,1)}, ...), condition=%wide.region_3.4_spmd, body=%wide.region_0.3_spmd.sunk | while | flops 211122688 | bytes 12907109 | solution.py:72
  183.8 4.0 copy.88
  187.8 3.7 all_to_all.26
  191.6 3.0 copy.89
  194.6 4.5 all-to-all-start
  199.7 1.6 copy.84
  201.3 1.7 copy.91
  203.0 33.6 %all-to-all-done = bf16[4,1024,192]{1,2,0:T(8,128)(2,1)} async-done(((bf16[4,1024,192]{1,2,0:T(8,128)(2,1)}), bf16[4,1024,192]{1,2,0:T(8,128)(2,1)}, u32[]{:S(2)}, u32[]{:S(2)}) %all-to-all-start) | async-done | bytes 1572896 | tf_op jit(solution)/shard_map/all_to_all | solution.py:178
  236.6 3.7 fusion.38
  241.1 11.4 %multiply_convert_fusion.1 = (bf16[1024,3072]{1,0:T(8,128)(2,1)}, f32[1024,3072]{1,0:T(8,128)}) fusion(f32[3072]{0:T(1024)S(1)} %copy-done.23, bf16[768,3072]{1,0:T(8,128)(2,1)S(1)} %bitcast.190, f32[1024,768]{0,1:T(8,128)S(1)} %get-tuple-element.284, f32[768]{0:T(1024)S(1)} %copy-done.26, f32[768]{0:T(1024)S(1)} %copy-done.21, ...), kind=kOutput, calls=%fused_computation.45 | convolution fusion | flops 4854644736 | bytes 26765312 | tf_op jit(solution)/shard_map/dot_general | solution.py:183
  252.5 7.7 fusion.39
  262.3 2.6 convert_reduce_fusion.2
  264.9 14.1 %convert_reduce_fusion = (f32[3072]{0:T(1024)S(1)}, bf16[1024,3072]{1,0:T(8,128)(2,1)}) fusion(f32[1024,3072]{1,0:T(8,128)} %get-tuple-element.286, f32[3072]{0:T(1024)S(1)} %copy-done.23, bf16[1024,768]{0,1:T(8,128)(2,1)S(1)} %get-tuple-element.271, bf16[3072,768]{1,0:T(8,128)(2,1)S(1)} %bitcast.188), kind=kOutput, calls=%fused_computation.43 | convolution fusion | flops 4872729600 | bytes 25190400 | tf_op jit(solution)/shard_map/td,id->ti/dot_general | solution.py:195
  279.0 8.9 multiply_reduce_fusion.1
  290.7 39.3 %all_to_all.35 = bf16[1024,4,192]{0,2,1:T(8,128)(2,1)S(1)} all-to-all(bf16[1024,4,192]{0,2,1:T(8,128)(2,1)S(1)} %bitcast.180), channel_id=1, replica_groups=mesh['rows'=8,'heads'=4] {'heads'}, dimensions={1} | all-to-all | bytes 3145728 | tf_op jit(solution)/shard_map/all_to_all | solution.py:215
  331.2 1.9 reshape.281
  333.1 3.1 copy.96
  338.9 78.3 %while.27 = (s32[]{:T(128)}, bf16[8,512,192]{1,2,0:T(8,128)(2,1)S(1)}, bf16[8,512,192]{1,2,0:T(8,128)(2,1)}, bf16[8,512,192]{1,2,0:T(8,128)(2,1)}, bf16[8,512,19...) while((s32[]{:T(128)}, ...), condition=%wide.region_14.15_spmd, body=%wide.region_12.14_spmd.sunk | while | flops 511146496 | bytes 28873352 | solution.py:122
  417.2 1.7 copy.120
  420.3 6.4 fusion.41
  426.7 6.3 fusion.42
  433.1 12.1 %add_convert_fusion = bf16[4096,768]{0,1:T(8,128)(2,1)} fusion(f32[4096,768]{0,1:T(8,128)} %fusion.41, f32[4096,768]{0,1:T(8,128)} %fusion.42, bf16[4096,192]{0,1:T(8,128)(2,1)S(1)} %bitcast.173, bf16[768,192]{0,1:T(8,128)(2,1)S(1)} %copy-done.14), kind=kOutput, calls=%fused_computation.44 | convolution fusion | flops 1217396736 | bytes 33325056 | tf_op jit(solution)/shard_map/tc,dc->td/dot_general | solution.py:225
  445.5 5.3 fusion.30
  450.9 5.9 convolution_bitcast_fusion
  456.8 5.2 convolution_bitcast_fusion.1
  462.0 2.2 convolution_bitcast_fusion.2
  464.3 11.0 %fusion.33 = f32[768,3072]{0,1:T(8,128)} fusion(bf16[1024,3072]{1,0:T(8,128)(2,1)} %get-tuple-element.291, f32[1024,768]{0,1:T(8,128)} %copy-done.2, f32[768]{0:T(1024)S(1)} %copy-done.26, f32[768]{0:T(1024)S(1)} %copy-done.21, f32[1024]{0:T(1024)S(1)} %add_rsqrt_fusion.1, f32[1024]{0:T(1024)S(1)} %broadcast_multiply_fusion.5), kind=kOutput, calls=%fused_computation.100 | convolution fusion | flops 4835770368 | bytes 18888704 | tf_op jit(solution)/shard_map/td,ti->di/dot_general | solution.py:197
  475.4 9.9 fusion.43
  485.2 2.6 copy.104
  487.8 50.4 %all-reduce.1 = (f32[768]{0:T(1024)}, f32[768]{0:T(1024)}, f32[768]{0:T(1024)}, f32[3072]{0:T(1024)S(1)}, f32[768]{0:T(1024)}, /*index=5*/f32[768]{0:T(1024)}, f32[768]{0:T(1024)}) all-reduce(f32[768]{0:T(1024)S(1)} %get-tuple-element.272, f32[768]{0:T(1024)S(1)} %get-tuple-element.216, ...), channel_id=1, replica_groups=mesh['rows'=8,'heads'=4] {'rows','heads'}, use_global_device_ids=true, to_apply=%region_25.26 | all-reduce | flops 7680 | bytes 61440 | tf_op jit(solution)/shard_map/psum | solution.py:249
  538.8 1.8 convert_reduce_fusion.4
  540.9 13.6 %all-reduce.2 = (f32[192]{0:T(256)}, f32[192]{0:T(256)}) all-reduce(f32[192]{0:T(256)S(1)} %convert_reduce_fusion.5, f32[192]{0:T(256)S(1)} %convert_reduce_fusion.4), channel_id=1, replica_groups=mesh['rows'=8,'heads'=4] {'rows'}, use_global_device_ids=true, to_apply=%region_20.21 | all-reduce | flops 384 | bytes 3072 | tf_op jit(solution)/shard_map/psum | solution.py:238
  554.5 1.7 reduce-scatter.4.cloned.1.call-done
  556.2 4.8 convert_add_fusion
  561.0 3.5 copy.105
  564.5 133.3 %all-reduce.7.cloned.1.call-done = f32[768,768]{1,0:T(8,128)} async-done(((f32[768,768]{1,0:T(8,128)}), f32[768,768]{1,0:T(8,128)}) %all-reduce.7.cloned.1.call-update) | async-done | bytes 2359312 | tf_op jit(solution)/shard_map/psum | solution.py:249
  697.8 63.8 %all-reduce.9.cloned.1.call-done = (f32[768,192]{0,1:T(8,128)}, f32[768,192]{0,1:T(8,128)}, f32[768,192]{0,1:T(8,128)}) async-done(((f32[768,192]{0,1:T(8,128)}, f32[768,192]{0,1:T(8,128)}, f32[768,192]{0,1:T(8,128)}), (f32[768,192]{0,1:T(8,128)}, f32[768,192]{0,1:T(8,128)}, f32[768,192]{0,1:T(8,128)})) %all-reduce.9.cloned.1.call-update) | async-done | bytes 1769488 | tf_op jit(solution)/shard_map/psum | solution.py:238
  761.6 141.2 %reduce-scatter.6.cloned.1.call-done = f32[768,96]{0,1:T(8,128)} async-done(((f32[768,3072]{0,1:T(8,128)}), f32[768,96]{0,1:T(8,128)}) %reduce-scatter.6.cloned.1.call-update) | async-done | bytes 294928 | tf_op jit(solution)/shard_map/reduce_scatter | solution.py:262
  902.8 141.9 %reduce-scatter.8.cloned.1.call-done = f32[96,768]{1,0:T(8,128)} async-done(((f32[3072,768]{1,0:T(8,128)}), f32[96,768]{1,0:T(8,128)}) %reduce-scatter.8.cloned.1.call-update) | async-done | bytes 294928 | tf_op jit(solution)/shard_map/reduce_scatter | solution.py:263
  1044.7 1.9 copy.157
  1046.6 2.0 copy.158
  1048.6 1.9 copy.159
  1050.6 1.4 copy.160
  (299 shorter events, 137.1 us)
Async XLA Ops:
  7.2 229.4 %copy-start = (bf16[768,768]{1,0:T(8,128)(2,1)S(1)}, bf16[768,768]{1,0:T(8,128)(2,1)}, u32[]{:S(2)}) copy-start(bf16[768,768]{1,0:T(8,128)(2,1)} %param.29) | copy-start | bytes 3538948
  7.2 120.5 %all-gather.2.cloned.1.call-start = ((), (), s32[]{:S(2)}) async-start(), calls=%async_computation.5 | async-start | bytes 7864320 | tf_op jit(solution)/shard_map/all_gather | solution.py:173
  127.7 5.3 copy-start.22
  132.8 1.0 copy-start.17
  133.8 2.2 copy-start.15
  183.8 7.7 copy-start.4
  194.6 5.1 copy-start.10
  194.6 42.0 %all-to-all-start = ((bf16[4,1024,192]{1,2,0:T(8,128)(2,1)}), bf16[4,1024,192]{1,2,0:T(8,128)(2,1)}, u32[]{:S(2)}, u32[]{:S(2)}) async-start(bf16[4,1024,192]{1,2,0:T(8,128)(2,1)} %copy.89), calls=%async_computation | async-start | bytes 3145728 | tf_op jit(solution)/shard_map/all_to_all | solution.py:178
  199.1 37.5 %copy-start.24 = (f32[768]{0:T(1024)S(1)}, f32[768]{0:T(1024)}, u32[]{:S(2)}) copy-start(f32[768]{0:T(1024)} %param.30) | copy-start | bytes 9220
  199.1 357.1 %reduce-scatter.4.cloned.1.call-start = ((), (), s32[]{:S(2)}) async-start(), calls=%async_computation.6 | async-start | bytes 7864320 | tf_op jit(solution)/shard_map/reduce_scatter | solution.py:221
  236.6 4.2 slice-start.4
  236.6 4.2 slice-start.5
  240.3 47.6 %copy-start.2 = (f32[1024,768]{0,1:T(8,128)}, f32[1024,768]{0,1:T(8,128)S(1)}, u32[]{:S(2)}) copy-start(f32[1024,768]{0,1:T(8,128)S(1)} %get-tuple-element.284) | copy-start | bytes 9437188
  240.3 0.7 copy-start.21
  240.3 0.8 copy-start.23
  240.3 0.8 copy-start.26
  240.4 12.2 %slice-start.2 = ((s8[4718592]{0:T(1024)(128)(4,1)}), s8[4194304]{0:T(1024)(128)(4,1)S(1)}, s32[]{:S(2)}) async-start(s8[4718592]{0:T(1024)(128)(4,1)} %bitcast.187), calls=%async_computation.13 | async-start | bytes 8388608
  241.1 11.4 %slice-start.3 = ((s8[4718592]{0:T(1024)(128)(4,1)}), s8[524288]{0:T(1024)(128)(4,1)S(1)}, s32[]{:S(2)}) async-start(s8[4718592]{0:T(1024)(128)(4,1)} %bitcast.187), calls=%async_computation.14 | async-start | bytes 1048576
  241.1 11.4 %copy-start.25 = (f32[768]{0:T(1024)S(1)}, f32[768]{0:T(1024)}, u32[]{:S(2)}) copy-start(f32[768]{0:T(1024)} %param.36) | copy-start | bytes 9220
  260.2 0.7 copy-start.19
  260.6 1.7 copy-start.20
  264.9 14.1 %copy-start.13 = (bf16[1024,768]{0,1:T(8,128)(2,1)}, bf16[1024,768]{0,1:T(8,128)(2,1)S(1)}, u32[]{:S(2)}) copy-start(bf16[1024,768]{0,1:T(8,128)(2,1)S(1)} %get-tuple-element.271) | copy-start | bytes 4718596
  289.1 1.7 copy-start.3
  417.2 1.9 copy-start.11
  418.9 14.1 %copy-start.9 = (bf16[8,24,8,512]{3,2,0,1:T(8,128)(2,1)}, bf16[8,24,8,512]{3,2,0,1:T(8,128)(2,1)S(1)}, u32[]{:S(2)}) copy-start(bf16[8,24,8,512]{3,2,0,1:T(8,128)(2,1)S(1)} %copy.120) | copy-start | bytes 4718596
  419.1 1.2 copy-start.16
  419.3 7.4 copy-start.5
  419.5 7.3 copy-start.7
  420.3 6.4 copy-start.18
  426.7 6.3 copy-start.14
  445.2 252.6 %all-reduce.7.cloned.1.call-start = ((), (), s32[]{:S(2)}) async-start(), calls=%async_computation.7 | async-start | bytes 4718592 | tf_op jit(solution)/shard_map/psum | solution.py:249
  450.8 310.8 %all-reduce.9.cloned.1.call-start = ((), (), s32[]{:S(2)}) async-start(), calls=%async_computation.10 | async-start | bytes 3538944 | tf_op jit(solution)/shard_map/psum | solution.py:238
  450.9 5.9 copy-start.6
  450.9 11.1 %slice-start = ((s8[6291456]{0:T(1024)(128)(4,1)}), s8[4194304]{0:T(1024)(128)(4,1)S(1)}, s32[]{:S(2)}) async-start(s8[6291456]{0:T(1024)(128)(4,1)} %bitcast.185), calls=%async_computation.11 | async-start | bytes 8388608
  456.8 5.2 copy-start.8
  456.8 5.2 slice-start.1
  464.3 438.5 %reduce-scatter.6.cloned.1.call-start = ((), (), s32[]{:S(2)}) async-start(), calls=%async_computation.8 | async-start | bytes 9732096 | tf_op jit(solution)/shard_map/reduce_scatter | solution.py:262
  475.3 569.4 %reduce-scatter.8.cloned.1.call-start = ((), (), s32[]{:S(2)}) async-start(), calls=%async_computation.9 | async-start | bytes 9732096 | tf_op jit(solution)/shard_map/reduce_scatter | solution.py:263
  697.8 352.8 %copy-start.12 = (f32[768,768]{1,0:T(8,128)S(1)}, f32[768,768]{1,0:T(8,128)}, u32[]{:S(2)}) copy-start(f32[768,768]{1,0:T(8,128)} %all-reduce.7.cloned.1.call-done) | copy-start | bytes 7077892
  1046.6 5.3 copy-start.1
Sparse Core Ops, SparseCore 0:
  9.6 118.0 all-gather.1
  445.3 110.8 reduce-scatter.3
  562.3 135.4 all-reduce.6
  702.2 59.3 all-reduce.8
  768.0 134.7 reduce-scatter.5
  910.1 134.5 reduce-scatter.7
where the time goes:
time: 1070 us; the launch traced here: 1060 us
  waiting for transfers between devices  635 us (59%)
  matrix products  162 us (15%)
  local copies, waits for them, and re-layouts  108 us (10%)
  blocking collectives  103 us (10%)
  other arithmetic  30 us (3%)
  between operations  15.1 us (1%)
    reduce_scatter x1, waiting for transfers between devices, local(): lax.psum_scatter(grad_w_outer, ('rows', 'heads'), scatter_dimension=0, ti...  142 us
    reduce_scatter x1, waiting for transfers between devices, local(): lax.psum_scatter(grad_w_inner, ('rows', 'heads'), scatter_dimension=1, ti...  141 us
    psum x1, waiting for transfers between devices, local(): lax.psum((grad_w_output, grad_b_output, grad_gain_attn, grad_shift_attn,...  133 us
    all_gather x1, waiting for transfers between devices, local(): gathered = lax.all_gather(layer_in, 'heads', axis=0, tiled=True)  118 us
    psum x1, waiting for transfers between devices, local(): lax.psum((grad_w_query, grad_w_key, grad_w_value, grad_b_query, grad_b_va...  63.8 us
    dynamic_slice x64, local copies, waits for them, and re-layouts, attend_forward(): lax.map(one_sequence, (query.reshape(count_seq, length, -1), keys_all.res...  50.5 us
    psum x1, blocking collectives, local(): lax.psum((grad_w_output, grad_b_output, grad_gain_attn, grad_shift_attn,...  50.4 us
    all_to_all x1, blocking collectives, local(): lax.all_to_all(grad_context_tok, 'heads', split_axis=1, concat_axis=0, ti...  39.3 us
  transfers between devices with their start and end apart: 7, of which 7 were waited for; matrix products, arithmetic and copies ran while one was open for 5% of the time, Pallas kernels for 0%

commit v1 on v0

--- a/solution.py
+++ b/solution.py
@@ -138,18 +138,128 @@
     )
 
 
-def project_tokens(layer_in, query_full, key_full, value_full, bias_query, bias_value):
-    query_tok = (
-        jnp.dot(layer_in, query_full, preferred_element_type=jnp.float32) + bias_query
-    ).astype(jnp.bfloat16)
-    keys_tok = jnp.dot(layer_in, key_full, preferred_element_type=jnp.float32).astype(jnp.bfloat16)
-    values_tok = (
-        jnp.dot(layer_in, value_full, preferred_element_type=jnp.float32) + bias_value
-    ).astype(jnp.bfloat16)
-    return (query_tok, keys_tok, values_tok)
+def bits_of(count):
+    return count.bit_length() - 1
+
+
+class Grid:
+    def __init__(self, mesh):
+        self.rows = mesh.shape["rows"]
+        self.heads = mesh.shape["heads"]
+        count = bits_of(self.rows) - 1
+        up = list(range(1, count + 1))
+        self.orders = (up, up[::-1])
+        self.steps = count
+
+    def permute(self, values, partner):
+        pairs = []
+        for row in range(self.rows):
+            for head in range(self.heads):
+                row_to, head_to = partner(row, head)
+                pairs.append((row * self.heads + head, row_to * self.heads + head_to))
+        return lax.ppermute(values, ("rows", "heads"), pairs)
+
+    def across_core(self, values):
+        return self.permute(values, lambda row, head: (row ^ 1, head))
+
+    def across_chip(self, values, step):
+        return self.permute(
+            values, lambda row, head: (row ^ (1 << self.orders[row & 1][step]), head)
+        )
+
+    def across_heads(self, values, offset):
+        return self.permute(values, lambda row, head: (row, head ^ offset))
+
+    def slot_masks(self, core):
+        last = self.steps - 1
+        masks = []
+        for slot in range(1 << self.steps):
+            mask = 0
+            for step in range(self.steps):
+                mask |= ((slot >> (last - step)) & 1) << self.orders[core][step]
+            masks.append(mask)
+        return masks
+
+    def row_slots(self):
+        row = lax.axis_index("rows")
+        masks = jnp.array([self.slot_masks(0), self.slot_masks(1)], jnp.int32)
+        core = row & 1
+        return jnp.stack([row ^ masks[core], (row ^ 1) ^ masks[1 - core]]).reshape(-1)
+
+    def head_slots(self):
+        return lax.axis_index("heads") ^ jnp.arange(self.heads, dtype=jnp.int32)
+
+    def block_slots(self):
+        return (self.row_slots()[:, None] * self.heads + self.head_slots()[None, :]).reshape(-1)
+
+    def reduce_scatter(self, parts):
+        held = parts.reshape((2, self.rows // 2) + parts.shape[1:])
+        held = add_low(held[0], self.across_core(held[1]))
+        for step in range(self.steps):
+            half = held.shape[0] // 2
+            held = add_low(held[:half], self.across_chip(held[half:], step))
+        held = held[0]
+        total = held[0].astype(jnp.float32)
+        for offset in range(1, self.heads):
+            total = total + self.across_heads(held[offset], offset).astype(jnp.float32)
+        return total
+
+    def gather_rows(self, block):
+        held = block[None]
+        for step in reversed(range(self.steps)):
+            held = jnp.concatenate([held, self.across_chip(held, step)], 0)
+        held = jnp.concatenate([held, self.across_core(held)], 0)
+        order = self.row_slots()
+        places = jnp.argsort(order)
+        return jnp.take(held, places, axis=0)
+
+    def gather_heads(self, block):
+        return jnp.stack(
+            [block] + [self.across_heads(block, offset) for offset in range(1, self.heads)]
+        )
+
+    def sum_all(self, values):
+        values = values + self.across_core(values)
+        for step in range(self.steps):
+            values = values + self.across_chip(values, step)
+        offset = 1
+        while offset < self.heads:
+            values = values + self.across_heads(values, offset)
+            offset *= 2
+        return values
+
+
+def add_low(first, second):
+    return (first.astype(jnp.float32) + second.astype(jnp.float32)).astype(jnp.bfloat16)
+
+
+def dot32(spec, left, right):
+    return jnp.einsum(spec, left, right, preferred_element_type=jnp.float32)
+
+
+def gather_projections(grid, shard):
+    helpers = 8
+    row = lax.axis_index("rows")
+    size = shard.shape[0] // helpers
+    part = lax.dynamic_slice_in_dim(shard, (row % helpers) * size, size, 0)
+    held = grid.gather_heads(part)[None]
+    for core_bit, other_bit in ((1, 2), (2, 1)):
+        got = grid.permute(
+            held, lambda r, h, b=core_bit, o=other_bit: (r ^ (1 << (o if r & 1 else b)), h)
+        )
+        held = jnp.concatenate([held, got], 0)
+    held = jnp.concatenate([held, grid.across_core(held)], 0)
+    core = row & 1
+    masks = jnp.array([[0, 2, 4, 6], [0, 4, 2, 6]], jnp.int32)
+    order = (
+        jnp.concatenate([row ^ masks[core], (row ^ 1) ^ masks[1 - core]]) % helpers
+    )
+    held = jnp.take(held, jnp.argsort(order), axis=0)
+    return held.transpose(1, 0, 2, 3).reshape(grid.heads, shard.shape[0], shard.shape[1])
 
 
 def local(
+    grid,
     layer_in,
     segment_ids,
     w_query,
@@ -170,19 +280,47 @@
     cotangent,
 ):
     scaling = HD ** (-0.5)
-    gathered = lax.all_gather(layer_in, "heads", axis=0, tiled=True)
-    query, keys_all, values_all = project_tokens(
-        gathered, w_query, w_key, w_value, b_query, b_value
-    )
-    context, log_sums = attend_forward(query, keys_all, values_all, segment_ids, scaling)
-    context_tok = lax.all_to_all(context, "heads", split_axis=0, concat_axis=1, tiled=True)
+    tokens, width = layer_in.shape
+    length = segment_ids.shape[1]
+    seqs = tokens // length
+    group = w_query.shape[1]
+    hidden = w_inner.shape[1]
+    devices = grid.rows * grid.heads
+    head = lax.axis_index("heads")
+    segments = lax.dynamic_slice_in_dim(segment_ids, head * seqs, seqs, 0)
+    slots = grid.block_slots()
+    head_slots = grid.head_slots()
+
+    shard = jnp.concatenate([w_query, w_key, w_value], 1).T
+    shard = jnp.concatenate([shard, jnp.zeros((0, width), shard.dtype)], 0)
+    projections = gather_projections(grid, shard).reshape(grid.heads, 3, group, width)
+    biases = jnp.stack([b_query, b_value])
+    biases = grid.gather_heads(biases)
+    w_query_all = projections[:, 0].reshape(-1, width)
+    w_key_all = projections[:, 1].reshape(-1, width)
+    w_value_all = projections[:, 2].reshape(-1, width)
+    b_query_all = biases[:, 0].reshape(-1)
+    b_value_all = biases[:, 1].reshape(-1)
+
+    def by_slot(values, block):
+        return jnp.take(values.reshape((devices, block) + values.shape[1:]), slots, axis=0).reshape(values.shape)
+
+    w_inner_t = by_slot(w_inner.T, hidden // devices)
+    w_outer_s = by_slot(w_outer, hidden // devices)
+    b_inner_s = by_slot(b_inner, hidden // devices)
+    w_output_s = jnp.take(w_output.reshape(grid.heads, group, width), head_slots, axis=0).reshape(width, width)
+
+    query = (dot32("td,cd->tc", layer_in, w_query_all) + b_query_all).astype(jnp.bfloat16)
+    keys_all = dot32("td,cd->tc", layer_in, w_key_all).astype(jnp.bfloat16)
+    values_all = (dot32("td,cd->tc", layer_in, w_value_all) + b_value_all).astype(jnp.bfloat16)
+    context, log_sums = attend_forward(query, keys_all, values_all, segments, scaling)
     inputs_wide = layer_in.astype(jnp.float32)
-    branch = jnp.dot(context_tok, w_output, preferred_element_type=jnp.float32) + b_output
+    branch = dot32("tc,cd->td", context, w_output_s) + b_output
     normed, normal_one, rstd_one = norm_forward(inputs_wide + branch, gain_attn, shift_attn)
     normed_low = normed.astype(jnp.bfloat16)
-    inner_pre = jnp.dot(normed_low, w_inner, preferred_element_type=jnp.float32) + b_inner
+    inner_pre = dot32("td,id->ti", normed_low, w_inner_t) + b_inner_s
     active = gelu_value(inner_pre).astype(jnp.bfloat16)
-    outer_out = jnp.dot(active, w_outer, preferred_element_type=jnp.float32) + b_outer
+    outer_out = dot32("ti,id->td", active, w_outer_s) + b_outer
     result, normal_two, rstd_two = norm_forward(normed + outer_out, gain_ffn, shift_ffn)
     layer_out = result.astype(jnp.bfloat16)
     grad_result = cotangent.astype(jnp.float32)
@@ -191,103 +329,99 @@
     grad_sum_two = norm_backward(grad_result, normal_two, rstd_two, gain_ffn)
     grad_outer = grad_sum_two.astype(jnp.bfloat16)
     grad_b_outer = jnp.sum(grad_outer.astype(jnp.float32), 0)
-    grad_w_outer = jnp.einsum("ti,td->id", active, grad_outer, preferred_element_type=jnp.float32)
-    grad_active = jnp.einsum("td,id->ti", grad_outer, w_outer, preferred_element_type=jnp.float32)
+    block_shape = (grid.rows, grid.heads, hidden // devices, width)
+    grad_w_outer = dot32("ti,td->id", active, grad_outer).astype(jnp.bfloat16)
+    out_w_outer = grid.reduce_scatter(grad_w_outer.reshape(block_shape))
+    grad_active = dot32("td,id->ti", grad_outer, w_outer_s)
     grad_inner = (grad_active * gelu_slope(inner_pre)).astype(jnp.bfloat16)
-    grad_w_inner = jnp.einsum(
-        "td,ti->di", normed_low, grad_inner, preferred_element_type=jnp.float32
-    )
+    grad_w_inner = dot32("ti,td->id", grad_inner, normed_low).astype(jnp.bfloat16)
+    out_w_inner = grid.reduce_scatter(grad_w_inner.reshape(block_shape)).T
     grad_b_inner = jnp.sum(grad_inner.astype(jnp.float32), 0)
-    grad_normed = grad_sum_two + jnp.einsum(
-        "ti,di->td", grad_inner, w_inner, preferred_element_type=jnp.float32
-    )
+    grad_normed = grad_sum_two + dot32("ti,id->td", grad_inner, w_inner_t)
     grad_gain_attn = jnp.sum(grad_normed * normal_one, 0)
     grad_shift_attn = jnp.sum(grad_normed, 0)
     grad_sum_one = norm_backward(grad_normed, normal_one, rstd_one, gain_attn)
     grad_branch = grad_sum_one.astype(jnp.bfloat16)
     grad_b_output = jnp.sum(grad_branch.astype(jnp.float32), 0)
-    grad_w_output = jnp.einsum(
-        "tc,td->cd", context_tok, grad_branch, preferred_element_type=jnp.float32
-    )
-    grad_context_tok = jnp.einsum(
-        "td,cd->tc", grad_branch, w_output, preferred_element_type=jnp.float32
+    grad_w_output = dot32("tc,td->cd", context, grad_branch)
+    grad_context = dot32("td,cd->tc", grad_branch, w_output_s).astype(jnp.bfloat16)
+    grad_query, grad_keys, grad_values = attend_backward(
+        query, keys_all, values_all, segments, log_sums, grad_context, scaling
+    )
+    input_grad = grad_sum_one + (
+        dot32("tc,cd->td", grad_query, w_query_all)
+        + dot32("tc,cd->td", grad_keys, w_key_all)
+        + dot32("tc,cd->td", grad_values, w_value_all)
+    )
+    four = jnp.stack(
+        [
+            dot32("tc,td->cd", grad_query, layer_in).reshape(grid.heads, group, width),
+            dot32("tc,td->cd", grad_keys, layer_in).reshape(grid.heads, group, width),
+            dot32("tc,td->cd", grad_values, layer_in).reshape(grid.heads, group, width),
+            grad_w_output.reshape(grid.heads, group, width),
+        ],
+        1,
     ).astype(jnp.bfloat16)
-    grad_context = lax.all_to_all(
-        grad_context_tok, "heads", split_axis=1, concat_axis=0, tiled=True
-    )
-    grad_query, grad_keys, grad_values = attend_backward(
-        query, keys_all, values_all, segment_ids, log_sums, grad_context, scaling
-    )
-    grad_heads_in = lax.psum_scatter(
-        (
-            jnp.einsum("tc,dc->td", grad_query, w_query, preferred_element_type=jnp.float32)
-            + jnp.einsum("tc,dc->td", grad_keys, w_key, preferred_element_type=jnp.float32)
-            + jnp.einsum("tc,dc->td", grad_values, w_value, preferred_element_type=jnp.float32)
-        ).astype(jnp.bfloat16),
-        "heads",
-        scatter_dimension=0,
-        tiled=True,
-    ).astype(jnp.float32)
-    grad_w_query = jnp.einsum("td,tc->dc", gathered, grad_query, preferred_element_type=jnp.float32)
-    grad_w_key = jnp.einsum("td,tc->dc", gathered, grad_keys, preferred_element_type=jnp.float32)
-    grad_w_value = jnp.einsum(
-        "td,tc->dc", gathered, grad_values, preferred_element_type=jnp.float32
-    )
-    grad_b_query = jnp.sum(grad_query.astype(jnp.float32), 0)
-    grad_b_value = jnp.sum(grad_values.astype(jnp.float32), 0)
-    grad_w_query, grad_w_key, grad_w_value, grad_b_query, grad_b_value = lax.psum(
-        (grad_w_query, grad_w_key, grad_w_value, grad_b_query, grad_b_value), "rows"
-    )
-    (
-        grad_w_output,
-        grad_b_output,
-        grad_gain_attn,
-        grad_shift_attn,
-        grad_b_outer,
-        grad_gain_ffn,
-        grad_shift_ffn,
-    ) = lax.psum(
-        (
-            grad_w_output,
-            grad_b_output,
-            grad_gain_attn,
-            grad_shift_attn,
-            grad_b_outer,
-            grad_gain_ffn,
-            grad_shift_ffn,
-        ),
-        ("rows", "heads"),
-    )
-    grad_w_inner, grad_w_outer, grad_b_inner = (
-        lax.psum_scatter(grad_w_inner, ("rows", "heads"), scatter_dimension=1, tiled=True),
-        lax.psum_scatter(grad_w_outer, ("rows", "heads"), scatter_dimension=0, tiled=True),
-        lax.psum_scatter(grad_b_inner, ("rows", "heads"), scatter_dimension=0, tiled=True),
-    )
-    input_grad = grad_sum_one + grad_heads_in
+    per_row = group // grid.rows
+    four = four.reshape(grid.heads, 4, grid.rows, per_row, width).transpose(2, 0, 1, 3, 4)
+    four = jnp.take(four, grid.row_slots(), axis=0)
+    four = grid.reduce_scatter(four.reshape(grid.rows, grid.heads, 4 * per_row, width)).astype(jnp.bfloat16)
+    four = grid.gather_rows(four).reshape(grid.rows, 4, per_row, width)
+    four = four.transpose(1, 0, 2, 3).reshape(4, group, width)
+    own_output = four[3]
+    grad_w_output = jnp.take(grid.gather_heads(own_output), head_slots, axis=0).reshape(width, width)
+    grad_w_output = grad_w_output.astype(jnp.float32)
+    wide = four[:3].astype(jnp.float32).transpose(0, 2, 1)
+
+    def back(values):
+        return jnp.take(values.reshape(grid.heads, group), head_slots, axis=0).reshape(1, width)
+
+    b_inner_back = jnp.take(
+        grad_b_inner.reshape(devices, hidden // devices), jnp.argsort(slots), axis=0
+    ).reshape(-1, width)
+    small = jnp.concatenate(
+        [
+            back(jnp.sum(grad_query.astype(jnp.float32), 0)),
+            back(jnp.sum(grad_values.astype(jnp.float32), 0)),
+            grad_b_output[None],
+            grad_gain_attn[None],
+            grad_shift_attn[None],
+            grad_b_outer[None],
+            grad_gain_ffn[None],
+            grad_shift_ffn[None],
+            b_inner_back,
+        ],
+        0,
+    )
+    small = grid.sum_all(small)
+    own_device = lax.axis_index("rows") * grid.heads + head
     return (
         layer_out,
         input_grad,
-        grad_w_query,
-        grad_w_key,
-        grad_w_value,
-        grad_b_query,
-        grad_b_value,
+        wide[0],
+        wide[1],
+        wide[2],
+        lax.dynamic_slice_in_dim(small[0], head * group, group, 0),
+        lax.dynamic_slice_in_dim(small[1], head * group, group, 0),
         grad_w_output,
-        grad_b_output,
-        grad_gain_attn,
-        grad_shift_attn,
-        grad_w_inner,
-        grad_b_inner,
-        grad_w_outer,
-        grad_b_outer,
-        grad_gain_ffn,
-        grad_shift_ffn,
+        small[2],
+        small[3],
+        small[4],
+        out_w_inner,
+        lax.dynamic_slice_in_dim(
+            small[8:].reshape(-1), own_device * (hidden // devices), hidden // devices, 0
+        ),
+        out_w_outer,
+        small[5],
+        small[6],
+        small[7],
     )
 
 
 def solution(mesh):
+    grid = Grid(mesh)
     return jax.shard_map(
-        local,
+        lambda *values: local(grid, *values),
         mesh=mesh,
         in_specs=(
             P(("rows", "heads"), None),

time: 1070 us -> 513 us (0.48)
  waiting for transfers between devices: 635 us -> 80.8 us
  blocking collectives: 103 us -> 0 us
  other arithmetic: 30 us -> 86.6 us
  starting transfers between devices: 5.52 us -> 48.9 us
  local copies, waits for them, and re-layouts: 108 us -> 123 us
  between operations: 15.1 us -> 1.96 us
    reduce_scatter x3 -> x0, waiting for transfers between devices: 285 us -> none  [the longest x1 142 us: local(): lax.psum_scatter(grad_w_outer, ('rows', 'heads'), scatter_dimension=0, ti...]
    psum x2 -> x0, waiting for transfers between devices: 197 us -> none  [the longest x1 133 us: local(): lax.psum((grad_w_output, grad_b_output, grad_gain_attn, grad_shift_attn,...]
    all_gather x1 -> x0, waiting for transfers between devices: 118 us -> none  [local(): gathered = lax.all_gather(layer_in, 'heads', axis=0, tiled=True)]
    ppermute x0 -> x38, waiting for transfers between devices: none -> 80.8 us  [permute(): return lax.ppermute(values, ('rows', 'heads'), pairs)]
    psum x2 -> x0, blocking collectives: 64 us -> none  [the longest x1 50.4 us: local(): lax.psum((grad_w_output, grad_b_output, grad_gain_attn, grad_shift_attn,...]
    ppermute x0 -> x38, starting transfers between devices: none -> 48.9 us  [permute(): return lax.ppermute(values, ('rows', 'heads'), pairs)]
    dynamic_slice x64 -> x18, local copies, waits for them, and re-layouts: 50.5 us -> 10.9 us  [attend_forward(): lax.map(one_sequence, (query.reshape(count_seq, length, -1), keys_all.res...]
    all_to_all x1 -> x0, blocking collectives: 39.3 us -> none  [local(): lax.all_to_all(grad_context_tok, 'heads', split_axis=1, concat_axis=0, ti...]
  transfers between devices with their start and end apart: 7 -> 38, of which waited for: 7 -> 13; matrix products, arithmetic and copies ran while one was open for 5% -> 47% of each run, Pallas kernels for 0% -> 0%
where the time goes in v1:
time: 513 us; the launch traced here: 503 us
  matrix products  161 us (31%)
  local copies, waits for them, and re-layouts  123 us (24%)
  other arithmetic  86.6 us (17%)
  waiting for transfers between devices  80.8 us (16%)
  starting transfers between devices  48.9 us (10%)
    dot_general x18, matrix products, dot32(): return jnp.einsum(spec, left, right, preferred_element_type=jnp.float32)  90.2 us
    ppermute x38, waiting for transfers between devices, permute(): return lax.ppermute(values, ('rows', 'heads'), pairs)  80.8 us
    ppermute x38, starting transfers between devices, permute(): return lax.ppermute(values, ('rows', 'heads'), pairs)  48.9 us
    unnamed x123, local copies, waits for them, and re-layouts  24.8 us
    dot_general x2, matrix products, one_sequence(): jnp.einsum('qhc,khc->hqk', grad_seq, values_seq, preferred_element_type=j...  22 us
    dot_general x4, matrix products, masked_scores(): jnp.einsum('qhc,khc->hqk', query_seq, keys_seq, preferred_element_type=jn...  17 us
    convert_element_type x9, other arithmetic, add_low(): (first.astype(jnp.float32) + second.astype(jnp.float32)).astype(jnp.bfloa...  15 us
    convert_element_type x2, other arithmetic, one_sequence(): grad_scores = (probs_full * (grad_probs - inner_sum)).astype(jnp.bfloat16)  14 us
  transfers between devices with their start and end apart: 38, of which 13 were waited for; matrix products, arithmetic and copies ran while one was open for 47% of the time, Pallas kernels for 0%

profile of v1, /device:TPU:0, one launch (start us, length us, event | category | flops | bytes accessed | tf_op | source)
XLA Modules:
  0.0 503.2 jit_solution(6052238122224508754)
XLA Ops:
  9.8 3.5 collective-permute-start.7
  16.3 6.6 %copy.102 = bf16[768,3072]{0,1:T(8,128)(2,1)} copy(bf16[768,3072]{1,0:T(8,128)(2,1)} %param.45) | data formatting | bytes 9437184 | tf_op args[11]
  22.9 5.3 %gather_fusion.4 = bf16[32,96,768]{2,1,0:T(8,128)(2,1)} fusion(bf16[32,96,768]{2,1,0:T(8,128)(2,1)} %bitcast.309, s32[1024]{0:T(1024)S(1)} %pad_clamp_fusion.3), kind=kCustom, calls=%fused_computation.1.clone | custom fusion | bytes 9437312 | tf_op jit(solution)/shard_map/jit(_take)/gather | solution.py:306
  28.2 5.4 %gather_fusion.6 = bf16[32,96,768]{2,1,0:T(8,128)(2,1)} fusion(bf16[32,96,768]{2,1,0:T(8,128)(2,1)} %bitcast.326, s32[1024]{0:T(1024)S(1)} %pad_clamp_fusion.3), kind=kCustom, calls=%fused_computation.5.clone | custom fusion | bytes 9437312 | tf_op jit(solution)/shard_map/jit(_take)/gather | solution.py:306
  41.3 5.3 %collective-permute-done.3 = bf16[1,4,72,768]{3,2,1,0:T(8,128)(2,1)S(1)} collective-permute-done((bf16[1,4,72,768]{3,2,1,0:T(8,128)(2,1)S(1)}, bf16[1,4,72,768]{3,2,1,0:T(8,128)(2,1)S(1)}, u32[]{:S(2)}, u32[]{:S(2)}) %collective-permute-start.3) | collective-permute-done | bytes 442400 | tf_op jit(solution)/shard_map/ppermute | solution.py:160
  49.6 10.2 %collective-permute-done.4 = bf16[2,4,72,768]{3,2,1,0:T(8,128)(2,1)S(1)} collective-permute-done((bf16[2,4,72,768]{3,2,1,0:T(8,128)(2,1)S(1)}, bf16[2,4,72,768]{3,2,1,0:T(8,128)(2,1)S(1)}, u32[]{:S(2)}, u32[]{:S(2)}) %collective-permute-start.4) | collective-permute-done | bytes 884768 | tf_op jit(solution)/shard_map/ppermute | solution.py:160
  63.1 6.9 %broadcast_select_fusion = (bf16[32,96,768]{2,1,0:T(8,128)(2,1)}, bf16[32,96,768]{2,1,0:T(8,128)(2,1)}) fusion(bf16[32,96,768]{2,1,0:T(8,128)(2,1)} %gather_fusion.6, pred[32]{0:T(512)(128)(4,1)S(1)} %compare_and_fusion.1, bf16[32,96,768]{2,1,0:T(8,128)(2,1)S(1)} %copy-done.5), kind=kLoop, calls=%fused_computation.70 | loop fusion | flops 4718592 | bytes 18874400 | tf_op jit(solution)/shard_map/jit(_take)/select_n | solution.py:306
  79.2 4.6 gather_fusion
  95.9 24.0 %while.26 = (s32[]{:T(128)}, bf16[2,512,768]{2,1,0:T(8,128)(2,1)}, f32[2,12,512,1]{2,1,3,0:T(8,128)}, bf16[2,512,768]{1,2,0:T(8,128)(2,1)S(1)}, s32[2,512]{1,0:T...) while((s32[]{:T(128)}, bf16[2,512,768]{2,1,0:T(8,128)(2,1)}, ...), condition=%wide.region_4.5_spmd, body=%wide.region_1.4_spmd.sunk | while | flops 843704320 | bytes 50019424 | solution.py:72
  103.2 3.6 fusion.166
  115.2 3.6 fusion.166
  120.0 4.0 fusion.96
  124.9 10.5 %multiply_convert_fusion.3 = (bf16[1024,3072]{1,0:T(8,128)(2,1)}, f32[1024,3072]{1,0:T(8,128)}) fusion(f32[3072]{0:T(1024)S(1)} %copy-done.42, bf16[3072,768]{1,0:T(8,128)(2,1)S(1)} %bitcast.330, f32[1024,768]{0,1:T(8,128)S(1)} %get-tuple-element.323, f32[768]{0:T(1024)S(1)} %copy-done.57, f32[768]{0:T(1024)S(1)} %copy-done.48, ...), kind=kOutput, calls=%fused_computation.56 | convolution fusion | flops 4854644736 | bytes 26765312 | tf_op jit(solution)/shard_map/td,id->ti/dot_general | solution.py:237
  135.4 7.7 %fusion.97 = (f32[1024]{0:T(1024)S(1)}, f32[1024,768]{0,1:T(8,128)S(1)}) fusion(f32[768]{0:T(1024)S(1)} %copy-done.56, bf16[1024,3072]{1,0:T(8,128)(2,1)} %get-tuple-element.324, bf16[3072,768]{1,0:T(8,128)(2,1)S(1)} %bitcast.333, f32[768]{0:T(1024)S(1)} %copy-done.57, f32[768]{0:T(1024)S(1)} %copy-done.48, f32[1024]{0:T(1024)S(1)} %add_rsqrt_fusion.1, ...), kind=kOutput, calls=%fused_computation.249 | convolution fusion | flops 4837342208 | bytes 17323008 | tf_op jit(solution)/shard_map/ti,id->td/dot_general | solution.py:237
  149.7 5.5 %convolution_convert_fusion = bf16[3072,768]{1,0:T(8,128)(2,1)S(1)} fusion(bf16[1024,3072]{1,0:T(8,128)(2,1)S(1)} %bitcast.372, bf16[1024,768]{0,1:T(8,128)(2,1)S(1)} %get-tuple-element.277), kind=kOutput, calls=%fused_computation.58 | convolution fusion | flops 4834197504 | bytes 12582912 | tf_op jit(solution)/shard_map/ti,td->id/dot_general | solution.py:237
  155.2 12.5 %convert_reduce_fusion = (f32[3072]{0:T(1024)}, bf16[1024,3072]{1,0:T(8,128)(2,1)S(1)}) fusion(f32[1024,3072]{1,0:T(8,128)} %get-tuple-element.325, f32[3072]{0:T(1024)S(1)} %copy-done.42, bf16[1024,768]{0,1:T(8,128)(2,1)S(1)} %get-tuple-element.277, bf16[3072,768]{1,0:T(8,128)(2,1)S(1)} %bitcast.334), kind=kOutput, calls=%fused_computation.55 | convolution fusion | flops 4872729600 | bytes 25190400 | tf_op jit(solution)/shard_map/td,id->ti/dot_general | solution.py:237
  170.4 7.6 %convolution_convert_fusion.1 = bf16[3072,768]{1,0:T(8,128)(2,1)} fusion(bf16[1024,3072]{1,0:T(8,128)(2,1)S(1)} %get-tuple-element.330, f32[1024,768]{0,1:T(8,128)S(1)} %get-tuple-element.323, f32[768]{0:T(1024)S(1)} %copy-done.57, f32[768]{0:T(1024)S(1)} %copy-done.48, f32[1024]{0:T(1024)S(1)} %add_rsqrt_fusion.1, f32[1024]{0:T(1024)S(1)} %broadcast_multiply_fusion.5), kind=kOutput, calls=%fused_computation.59 | convolution fusion | flops 4838129664 | bytes 14170112 | tf_op jit(solution)/shard_map/ti,td->id/dot_general | solution.py:237
  178.0 12.3 %multiply_reduce_fusion.1 = (f32[768]{0:T(1024)}, f32[1024]{0:T(1024)S(1)}, f32[1024]{0:T(1024)S(1)}, f32[768]{0:T(1024)}, f32[1024,768]{0,1:T(8,128)}) fusion(f32[1024,768]{0,1:T(8,128)S(1)} %get-tuple-element.323, f32[1024]{0:T(1024)S(1)} %add_rsqrt_fusion.1, f32[1024]{0:T(1024)S(1)} %broadcast_multiply_fusion.5, f32[768]{0:T(1024)S(1)} %copy-done.48, ...), kind=kOutput, calls=%fused_computation.83 | convolution fusion | flops 4845989888 | bytes 22065152 | tf_op jit(solution)/shard_map/ti,id->td/dot_general | solution.py:237
  196.0 4.6 convert_reduce_fusion.3
  207.1 98.3 %while.27 = (s32[]{:T(128)}, bf16[2,512,768]{1,2,0:T(8,128)(2,1)}, bf16[2,512,768]{2,1,0:T(8,128)(2,1)}, bf16[2,512,768]{1,2,0:T(8,128)(2,1)}, bf16[2,512,768]{1...) while((s32[]{:T(128)}, bf16[2,512,768]{1,2,0:T(8,128)(2,1)}, ...), condition=%wide.region_15.19_spmd, body=%wide.region_13.18_spmd.sunk | while | flops 2062673920 | bytes 224574416 | solution.py:122
  211.1 6.4 %fusion.177 = f32[12,512,512]{1,2,0:T(8,128)} fusion(bf16[512,12,64]{0,2,1:T(8,128)(2,1)S(1)} %bitcast.296, bf16[512,12,64]{0,2,1:T(8,128)(2,1)S(1)} %bitcast.294), kind=kOutput, calls=%fused_computation.250.clone.1 | convolution fusion | flops 402653184 | bytes 14155776 | tf_op jit(solution)/shard_map/while/body/eval_jaxpr/qhc,khc->hqk/dot_general | solution.py:43
  220.0 11.0 %multiply_reduce_fusion.7 = (f32[12,512]{1,0:T(8,128)S(1)}, f32[12,512,512]{1,2,0:T(8,128)}) fusion(f32[12,512,512]{1,2,0:T(8,128)} %fusion.177, f32[12,512]{1,0:T(8,128)S(1)} %dynamic-slice_bitcast_fusion.2, pred[512,512]{0,1:T(8,128)(4,1)S(1)} %broadcast_compare_fusion.5, bf16[512,12,64]{0,2,1:T(8,128)(2,1)S(1)} %bitcast.299, ...), kind=kOutput, calls=%fused_computation.28.clone.1 | convolution fusion | flops 418375680 | bytes 27049984 | tf_op jit(solution)/shard_map/while/body/eval_jaxpr/qhc,khc->hqk/dot_general | solution.py:96
  232.6 7.0 %multiply_convert_fusion.7 = bf16[12,512,512]{1,2,0:T(8,128)(2,1)S(1)} fusion(f32[12,512,512]{1,2,0:T(8,128)} %get-tuple-element.453, f32[12,512,512]{1,2,0:T(8,128)S(1)} %bitcast.293, f32[12,512]{1,0:T(8,128)S(1)} %get-tuple-element.454, f32[12,512]{1,0:T(8,128)S(1)} %dynamic-slice_bitcast_fusion.2, pred[512,512]{0,1:T(8,128)(4,1)S(1)} %broadcast_compare_fusion.5), kind=kLoop, calls=%fused_computation.27.clone.1 | loop fusion | flops 18874368 | bytes 31768576 | tf_op jit(solution)/shard_map/while/body/eval_jaxpr/convert_element_type | solution.py:106
  243.4 3.9 multiply_convert_fusion.8
  247.4 6.5 %fusion.178 = bf16[12,64,512]{2,1,0:T(8,128)(2,1)S(1)} fusion(bf16[512,12,64]{0,2,1:T(8,128)(2,1)S(1)} %bitcast.300, f32[12,512,512]{1,2,0:T(8,128)} %fusion.177, f32[12,512]{1,0:T(8,128)S(1)} %dynamic-slice_bitcast_fusion.2, pred[512,512]{0,1:T(8,128)(4,1)S(1)} %broadcast_compare_fusion.5), kind=kOutput, calls=%fused_computation.35.clone.1 | convolution fusion | flops 415629312 | bytes 14442496 | tf_op jit(solution)/shard_map/while/body/eval_jaxpr/hqk,qhc->khc/dot_general | solution.py:99
  260.0 6.4 %fusion.177 = f32[12,512,512]{1,2,0:T(8,128)} fusion(bf16[512,12,64]{0,2,1:T(8,128)(2,1)S(1)} %bitcast.296, bf16[512,12,64]{0,2,1:T(8,128)(2,1)S(1)} %bitcast.294), kind=kOutput, calls=%fused_computation.250.clone.1 | convolution fusion | flops 402653184 | bytes 14155776 | tf_op jit(solution)/shard_map/while/body/eval_jaxpr/qhc,khc->hqk/dot_general | solution.py:43
  269.0 11.0 %multiply_reduce_fusion.7 = (f32[12,512]{1,0:T(8,128)S(1)}, f32[12,512,512]{1,2,0:T(8,128)}) fusion(f32[12,512,512]{1,2,0:T(8,128)} %fusion.177, f32[12,512]{1,0:T(8,128)S(1)} %dynamic-slice_bitcast_fusion.2, pred[512,512]{0,1:T(8,128)(4,1)S(1)} %broadcast_compare_fusion.5, bf16[512,12,64]{0,2,1:T(8,128)(2,1)S(1)} %bitcast.299, ...), kind=kOutput, calls=%fused_computation.28.clone.1 | convolution fusion | flops 418375680 | bytes 27049984 | tf_op jit(solution)/shard_map/while/body/eval_jaxpr/qhc,khc->hqk/dot_general | solution.py:96
  281.6 7.0 %multiply_convert_fusion.7 = bf16[12,512,512]{1,2,0:T(8,128)(2,1)S(1)} fusion(f32[12,512,512]{1,2,0:T(8,128)} %get-tuple-element.453, f32[12,512,512]{1,2,0:T(8,128)S(1)} %bitcast.293, f32[12,512]{1,0:T(8,128)S(1)} %get-tuple-element.454, f32[12,512]{1,0:T(8,128)S(1)} %dynamic-slice_bitcast_fusion.2, pred[512,512]{0,1:T(8,128)(4,1)S(1)} %broadcast_compare_fusion.5), kind=kLoop, calls=%fused_computation.27.clone.1 | loop fusion | flops 18874368 | bytes 31768576 | tf_op jit(solution)/shard_map/while/body/eval_jaxpr/convert_element_type | solution.py:106
  292.4 3.9 multiply_convert_fusion.8
  296.3 6.5 %fusion.178 = bf16[12,64,512]{2,1,0:T(8,128)(2,1)S(1)} fusion(bf16[512,12,64]{0,2,1:T(8,128)(2,1)S(1)} %bitcast.300, f32[12,512,512]{1,2,0:T(8,128)} %fusion.177, f32[12,512]{1,0:T(8,128)S(1)} %dynamic-slice_bitcast_fusion.2, pred[512,512]{0,1:T(8,128)(4,1)S(1)} %broadcast_compare_fusion.5), kind=kOutput, calls=%fused_computation.35.clone.1 | convolution fusion | flops 415629312 | bytes 14442496 | tf_op jit(solution)/shard_map/while/body/eval_jaxpr/hqk,qhc->khc/dot_general | solution.py:99
  308.7 4.4 fusion.55
  318.4 4.3 fusion.61
  325.4 3.4 fusion.58
  331.3 5.4 %gather_fusion.1 = bf16[8,4,4,24,768]{4,3,1,2,0:T(8,128)(2,1)} fusion(bf16[8,4,4,24,768]{4,3,0,1,2:T(8,128)(2,1)} %maximum_bitcast_fusion, s32[1024]{0:T(1024)} %pad_clamp_fusion.2), kind=kCustom, calls=%fused_computation.9 | custom fusion | bytes 9437216 | tf_op jit(solution)/shard_map/jit(_take)/gather | solution.py:367
  349.7 4.9 fusion.93
  360.6 3.3 fusion.100
  382.5 3.7 add_add_fusion
  386.2 3.7 copy.125
  408.5 7.1 %collective-permute-done.11 = bf16[1,4,96,768]{3,2,1,0:T(8,128)(2,1)} collective-permute-done((bf16[1,4,96,768]{3,2,1,0:T(8,128)(2,1)}, bf16[1,4,96,768]{3,2,1,0:T(8,128)(2,1)}, u32[]{:S(2)}, u32[]{:S(2)}) %collective-permute-start.11) | collective-permute-done | bytes 589856 | tf_op jit(solution)/shard_map/ppermute | solution.py:160
  421.4 7.2 %collective-permute-done.27 = bf16[2,4,96,768]{3,2,1,0:T(8,128)(2,1)} collective-permute-done((bf16[2,4,96,768]{3,2,1,0:T(8,128)(2,1)}, bf16[2,4,96,768]{3,2,1,0:T(8,128)(2,1)}, u32[]{:S(2)}, u32[]{:S(2)}) %collective-permute-start.27) | collective-permute-done | bytes 1179680 | tf_op jit(solution)/shard_map/ppermute | solution.py:160
  432.6 10.6 %collective-permute-done.15 = bf16[1,96,768]{2,1,0:T(8,128)(2,1)S(1)} collective-permute-done((bf16[1,96,768]{2,1,0:T(8,128)(2,1)S(1)}, bf16[1,96,768]{2,1,0:T(8,128)(2,1)S(1)}, u32[]{:S(2)}, u32[]{:S(2)}) %collective-permute-start.15) | collective-permute-done | bytes 147488 | tf_op jit(solution)/shard_map/ppermute | solution.py:160
  443.2 4.0 collective-permute-start.16
  447.2 3.8 collective-permute-start.35
  455.9 4.1 collective-permute-done.36
  460.8 3.4 collective-permute-done.29
  464.2 8.2 %collective-permute-done.30 = bf16[96,768]{1,0:T(8,128)(2,1)S(1)} collective-permute-done((bf16[96,768]{1,0:T(8,128)(2,1)S(1)}, bf16[96,768]{1,0:T(8,128)(2,1)S(1)}, u32[]{:S(2)}, u32[]{:S(2)}) %collective-permute-start.30) | collective-permute-done | bytes 147488 | tf_op jit(solution)/shard_map/ppermute | solution.py:160
  480.5 5.7 %collective-permute-done.23 = bf16[192,768]{1,0:T(8,128)(2,1)S(1)} collective-permute-done((bf16[192,768]{1,0:T(8,128)(2,1)S(1)}, bf16[192,768]{1,0:T(8,128)(2,1)S(1)}, u32[]{:S(2)}, u32[]{:S(2)}) %collective-permute-start.23) | collective-permute-done | bytes 294944 | tf_op jit(solution)/shard_map/ppermute | solution.py:160
  486.2 13.8 %collective-permute-done.24 = bf16[192,768]{1,0:T(8,128)(2,1)S(1)} collective-permute-done((bf16[192,768]{1,0:T(8,128)(2,1)S(1)}, bf16[192,768]{1,0:T(8,128)(2,1)S(1)}, u32[]{:S(2)}, u32[]{:S(2)}) %collective-permute-start.24) | collective-permute-done | bytes 294944 | tf_op jit(solution)/shard_map/ppermute | solution.py:160
  (433 shorter events, 209.8 us)
Async XLA Ops:
  0.7 35.8 %copy-start = (bf16[768,768]{1,0:T(8,128)(2,1)S(1)}, bf16[768,768]{1,0:T(8,128)(2,1)}, u32[]{:S(2)}) copy-start(bf16[768,768]{1,0:T(8,128)(2,1)} %param.41) | copy-start | bytes 3538948
  1.8 36.3 %collective-permute-start = (bf16[72,768]{1,0:T(8,128)(2,1)S(1)}, bf16[72,768]{1,0:T(8,128)(2,1)S(1)}, u32[]{:S(2)}, u32[]{:S(2)}) collective-permute-start(bf16[72,768]{1,0:T(8,128)(2,1)S(1)} %bitcast.356), channel_id=1, source_target_pairs={{0,1},{1,0},{2,3},{3,2},{4,5},{5,4},{6,7},{7,6},{8,9},{9,8},{10,11... | collective-permute-start | bytes 331784 | tf_op jit(solution)/shard_map/ppermute | solution.py:160
  4.9 33.3 %collective-permute-start.1 = (bf16[72,768]{1,0:T(8,128)(2,1)S(1)}, bf16[72,768]{1,0:T(8,128)(2,1)S(1)}, u32[]{:S(2)}, u32[]{:S(2)}) collective-permute-start(bf16[72,768]{1,0:T(8,128)(2,1)S(1)} %bitcast.357), channel_id=1, source_target_pairs={{0,2},{1,3},{2,0},{3,1},{4,6},{5,7},{6,4},{7,5},{8,10},{9,11},{10,... | collective-permute-start | bytes 331784 | tf_op jit(solution)/shard_map/ppermute | solution.py:160
  7.5 30.7 %collective-permute-start.2 = (bf16[72,768]{1,0:T(8,128)(2,1)S(1)}, bf16[72,768]{1,0:T(8,128)(2,1)S(1)}, u32[]{:S(2)}, u32[]{:S(2)}) collective-permute-start(bf16[72,768]{1,0:T(8,128)(2,1)S(1)} %bitcast.358), channel_id=1, source_target_pairs={{0,3},{1,2},{2,1},{3,0},{4,7},{5,6},{6,5},{7,4},{8,11},{9,10},{10,... | collective-permute-start | bytes 331784 | tf_op jit(solution)/shard_map/ppermute | solution.py:160
  8.8 67.1 %collective-permute-start.6 = (bf16[2,192]{1,0:T(2,128)(2,1)S(1)}, bf16[2,192]{1,0:T(2,128)(2,1)S(1)}, u32[]{:S(2)}, u32[]{:S(2)}) collective-permute-start(bf16[2,192]{1,0:T(2,128)(2,1)S(1)} %pad_maximum_fusion.8), channel_id=1, source_target_pairs={{0,1},{1,0},{2,3},{3,2},{4,5},{5,4},{6,7},{7,6},{8,9},{9,8},{10,11... | collective-permute-start | bytes 2312 | tf_op jit(solution)/shard_map/ppermute | solution.py:160
  9.8 66.1 %collective-permute-start.7 = (bf16[2,192]{1,0:T(2,128)(2,1)S(1)}, bf16[2,192]{1,0:T(2,128)(2,1)S(1)}, u32[]{:S(2)}, u32[]{:S(2)}) collective-permute-start(bf16[2,192]{1,0:T(2,128)(2,1)S(1)} %pad_maximum_fusion.8), channel_id=1, source_target_pairs={{0,2},{1,3},{2,0},{3,1},{4,6},{5,7},{6,4},{7,5},{8,10},{9,11},{10,... | collective-permute-start | bytes 2312 | tf_op jit(solution)/shard_map/ppermute | solution.py:160
  16.0 20.4 %copy-start.43 = (s32[1024]{0:T(1024)}, s32[1024]{0:T(1024)S(1)}, u32[]{:S(2)}) copy-start(s32[1024]{0:T(1024)S(1)} %pad_clamp_fusion.4) | copy-start | bytes 12292
  38.0 25.0 %copy-start.44 = (pred[4]{0:T(512)(128)(4,1)}, pred[4]{0:T(512)(128)(4,1)S(1)}, u32[]{:S(2)}) copy-start(pred[4]{0:T(512)(128)(4,1)S(1)} %compare_and_fusion.2) | copy-start | bytes 16
  38.1 37.8 %collective-permute-start.8 = (bf16[2,192]{1,0:T(2,128)(2,1)S(1)}, bf16[2,192]{1,0:T(2,128)(2,1)S(1)}, u32[]{:S(2)}, u32[]{:S(2)}) collective-permute-start(bf16[2,192]{1,0:T(2,128)(2,1)S(1)} %pad_maximum_fusion.8), channel_id=1, source_target_pairs={{0,3},{1,2},{2,1},{3,0},{4,7},{5,6},{6,5},{7,4},{8,11},{9,10},{10,... | collective-permute-start | bytes 2312 | tf_op jit(solution)/shard_map/ppermute | solution.py:160
  38.2 8.4 %collective-permute-start.3 = (bf16[1,4,72,768]{3,2,1,0:T(8,128)(2,1)S(1)}, bf16[1,4,72,768]{3,2,1,0:T(8,128)(2,1)S(1)}, u32[]{:S(2)}, u32[]{:S(2)}) collective-permute-start(bf16[1,4,72,768]{3,2,1,0:T(8,128)(2,1)S(1)} %maximum_bitcast_fusion.1), channel_id=1, source_target_pairs={{0,8},{1,9},{2,10},{3,11},{4,20},{5,21},{6,22},{7,23},{8,0},{9,1},... | collective-permute-start | bytes 1327112 | tf_op jit(solution)/shard_map/ppermute | solution.py:160
  46.7 16.4 %copy-start.5 = (bf16[32,96,768]{2,1,0:T(8,128)(2,1)S(1)}, bf16[32,96,768]{2,1,0:T(8,128)(2,1)}, u32[]{:S(2)}) copy-start(bf16[32,96,768]{2,1,0:T(8,128)(2,1)} %gather_fusion.4) | copy-start | bytes 14155780
  46.7 13.1 %collective-permute-start.4 = (bf16[2,4,72,768]{3,2,1,0:T(8,128)(2,1)S(1)}, bf16[2,4,72,768]{3,2,1,0:T(8,128)(2,1)S(1)}, u32[]{:S(2)}, u32[]{:S(2)}) collective-permute-start(bf16[2,4,72,768]{3,2,1,0:T(8,128)(2,1)S(1)} %pad_maximum_fusion.4), channel_id=1, source_target_pairs={{0,16},{1,17},{2,18},{3,19},{4,12},{5,13},{6,14},{7,15},{8,24},{9,... | collective-permute-start | bytes 2654216 | tf_op jit(solution)/shard_map/ppermute | solution.py:160
  61.2 14.9 %collective-permute-start.5 = (bf16[4,4,72,768]{3,2,1,0:T(8,128)(2,1)}, bf16[4,4,72,768]{3,2,1,0:T(8,128)(2,1)}, u32[]{:S(2)}, u32[]{:S(2)}) collective-permute-start(bf16[4,4,72,768]{3,2,1,0:T(8,128)(2,1)} %pad_maximum_fusion.1), channel_id=1, source_target_pairs={{0,4},{1,5},{2,6},{3,7},{4,0},{5,1},{6,2},{7,3},{8,12},{9,13},{10,... | collective-permute-start | bytes 5308424 | tf_op jit(solution)/shard_map/ppermute | solution.py:160
  95.9 24.0 %copy-start.55 = (f32[768]{0:T(1024)S(1)}, f32[768]{0:T(1024)}, u32[]{:S(2)}) copy-start(f32[768]{0:T(1024)} %param.42) | copy-start | bytes 9220
  124.0 54.0 %copy-start.7 = (f32[1024,768]{0,1:T(8,128)}, f32[1024,768]{0,1:T(8,128)S(1)}, u32[]{:S(2)}) copy-start(f32[1024,768]{0,1:T(8,128)S(1)} %get-tuple-element.323) | copy-start | bytes 9437188
  192.8 182.8 %collective-permute-start.32 = (bf16[4,4,96,768]{3,2,1,0:T(8,128)(2,1)}, bf16[4,4,96,768]{3,2,1,0:T(8,128)(2,1)}, u32[]{:S(2)}, u32[]{:S(2)}) collective-permute-start(bf16[4,4,96,768]{3,2,1,0:T(8,128)(2,1)} %bitcast.100), channel_id=1, source_target_pairs={{0,4},{1,5},{2,6},{3,7},{4,0},{5,1},{6,2},{7,3},{8,12},{9,13},{10,... | collective-permute-start | bytes 7077896 | tf_op jit(solution)/shard_map/ppermute | solution.py:160
  220.0 12.6 %slice-start.2 = ((s8[12582912]{0:T(1024)(128)(4,1)}), s8[4194304]{0:T(1024)(128)(4,1)S(1)}, s32[]{:S(2)}) async-start(s8[12582912]{0:T(1024)(128)(4,1)} %bitcast.292), calls=%async_computation.2 | async-start | bytes 8388608 | tf_op jit(solution)/shard_map/while
  269.0 12.6 %slice-start.2 = ((s8[12582912]{0:T(1024)(128)(4,1)}), s8[4194304]{0:T(1024)(128)(4,1)S(1)}, s32[]{:S(2)}) async-start(s8[12582912]{0:T(1024)(128)(4,1)} %bitcast.292), calls=%async_computation.2 | async-start | bytes 8388608 | tf_op jit(solution)/shard_map/while
  344.2 26.1 %collective-permute-start.9 = (bf16[4,4,96,768]{3,2,1,0:T(8,128)(2,1)}, bf16[4,4,96,768]{3,2,1,0:T(8,128)(2,1)}, u32[]{:S(2)}, u32[]{:S(2)}) collective-permute-start(bf16[4,4,96,768]{3,2,1,0:T(8,128)(2,1)} %bitcast.70), channel_id=1, source_target_pairs={{0,4},{1,5},{2,6},{3,7},{4,0},{5,1},{6,2},{7,3},{8,12},{9,13},{10,... | collective-permute-start | bytes 7077896 | tf_op jit(solution)/shard_map/ppermute | solution.py:160
  349.1 5.5 %collective-permute-start.18 = (f32[12,768]{1,0:T(8,128)S(1)}, f32[12,768]{1,0:T(8,128)S(1)}, u32[]{:S(2)}, u32[]{:S(2)}) collective-permute-start(f32[12,768]{1,0:T(8,128)S(1)} %concatenate.41), channel_id=1, source_target_pairs={{0,4},{1,5},{2,6},{3,7},{4,0},{5,1},{6,2},{7,3},{8,12},{9,13},{10,... | collective-permute-start | bytes 110600 | tf_op jit(solution)/shard_map/ppermute | solution.py:160
  354.6 37.1 %collective-permute-start.26 = (bf16[4,4,96,768]{3,2,1,0:T(8,128)(2,1)}, bf16[4,4,96,768]{3,2,1,0:T(8,128)(2,1)}, u32[]{:S(2)}, u32[]{:S(2)}) collective-permute-start(bf16[4,4,96,768]{3,2,1,0:T(8,128)(2,1)} %bitcast.93), channel_id=1, source_target_pairs={{0,4},{1,5},{2,6},{3,7},{4,0},{5,1},{6,2},{7,3},{8,12},{9,13},{10,... | collective-permute-start | bytes 7077896 | tf_op jit(solution)/shard_map/ppermute | solution.py:160
  354.6 4.2 collective-permute-start.19
  358.8 5.1 %collective-permute-start.20 = (f32[12,768]{1,0:T(8,128)S(1)}, f32[12,768]{1,0:T(8,128)S(1)}, u32[]{:S(2)}, u32[]{:S(2)}) collective-permute-start(f32[12,768]{1,0:T(8,128)S(1)} %add.334), channel_id=1, source_target_pairs={{0,16},{1,17},{2,18},{3,19},{4,12},{5,13},{6,14},{7,15},{8,24},{9,... | collective-permute-start | bytes 110600 | tf_op jit(solution)/shard_map/ppermute | solution.py:160
  364.0 4.2 collective-permute-start.21
  368.1 23.5 %collective-permute-start.22 = (f32[12,768]{1,0:T(8,128)S(1)}, f32[12,768]{1,0:T(8,128)S(1)}, u32[]{:S(2)}, u32[]{:S(2)}) collective-permute-start(f32[12,768]{1,0:T(8,128)S(1)} %add.336), channel_id=1, source_target_pairs={{0,2},{1,3},{2,0},{3,1},{4,6},{5,7},{6,4},{7,5},{8,10},{9,11},{10,... | collective-permute-start | bytes 110600 | tf_op jit(solution)/shard_map/ppermute | solution.py:160
  374.2 22.4 %collective-permute-start.10 = (bf16[2,4,96,768]{3,2,1,0:T(8,128)(2,1)}, bf16[2,4,96,768]{3,2,1,0:T(8,128)(2,1)}, u32[]{:S(2)}, u32[]{:S(2)}) collective-permute-start(bf16[2,4,96,768]{3,2,1,0:T(8,128)(2,1)} %slice.249), channel_id=1, source_target_pairs={{0,8},{1,9},{2,10},{3,11},{4,20},{5,21},{6,22},{7,23},{8,0},{9,1},... | collective-permute-start | bytes 3538952 | tf_op jit(solution)/shard_map/ppermute | solution.py:160
  381.0 25.4 %collective-permute-start.33 = (bf16[2,4,96,768]{3,2,1,0:T(8,128)(2,1)}, bf16[2,4,96,768]{3,2,1,0:T(8,128)(2,1)}, u32[]{:S(2)}, u32[]{:S(2)}) collective-permute-start(bf16[2,4,96,768]{3,2,1,0:T(8,128)(2,1)} %slice.280), channel_id=1, source_target_pairs={{0,8},{1,9},{2,10},{3,11},{4,20},{5,21},{6,22},{7,23},{8,0},{9,1},... | collective-permute-start | bytes 3538952 | tf_op jit(solution)/shard_map/ppermute | solution.py:160
  396.0 32.6 %collective-permute-start.27 = (bf16[2,4,96,768]{3,2,1,0:T(8,128)(2,1)}, bf16[2,4,96,768]{3,2,1,0:T(8,128)(2,1)}, u32[]{:S(2)}, u32[]{:S(2)}) collective-permute-start(bf16[2,4,96,768]{3,2,1,0:T(8,128)(2,1)} %slice.269), channel_id=1, source_target_pairs={{0,8},{1,9},{2,10},{3,11},{4,20},{5,21},{6,22},{7,23},{8,0},{9,1},... | collective-permute-start | bytes 3538952 | tf_op jit(solution)/shard_map/ppermute | solution.py:160
  399.1 16.6 %collective-permute-start.11 = (bf16[1,4,96,768]{3,2,1,0:T(8,128)(2,1)}, bf16[1,4,96,768]{3,2,1,0:T(8,128)(2,1)}, u32[]{:S(2)}, u32[]{:S(2)}) collective-permute-start(bf16[1,4,96,768]{3,2,1,0:T(8,128)(2,1)} %slice.251), channel_id=1, source_target_pairs={{0,16},{1,17},{2,18},{3,19},{4,12},{5,13},{6,14},{7,15},{8,24},{9,... | collective-permute-start | bytes 1769480 | tf_op jit(solution)/shard_map/ppermute | solution.py:160
  408.4 24.0 %collective-permute-start.34 = (bf16[1,4,96,768]{3,2,1,0:T(8,128)(2,1)S(1)}, bf16[1,4,96,768]{3,2,1,0:T(8,128)(2,1)S(1)}, u32[]{:S(2)}, u32[]{:S(2)}) collective-permute-start(bf16[1,4,96,768]{3,2,1,0:T(8,128)(2,1)S(1)} %slice.282), channel_id=1, source_target_pairs={{0,16},{1,17},{2,18},{3,19},{4,12},{5,13},{6,14},{7,15},{8,24},{9,... | collective-permute-start | bytes 1769480 | tf_op jit(solution)/shard_map/ppermute | solution.py:160
  416.9 14.1 %collective-permute-start.12 = (bf16[96,768]{1,0:T(8,128)(2,1)S(1)}, bf16[96,768]{1,0:T(8,128)(2,1)S(1)}, u32[]{:S(2)}, u32[]{:S(2)}) collective-permute-start(bf16[96,768]{1,0:T(8,128)(2,1)S(1)} %get-tuple-element.307), channel_id=1, source_target_pairs={{0,1},{1,0},{2,3},{3,2},{4,5},{5,4},{6,7},{7,6},{8,9},{9,8},{10,11... | collective-permute-start | bytes 442376 | tf_op jit(solution)/shard_map/ppermute | solution.py:160
  419.0 12.0 %collective-permute-start.13 = (bf16[96,768]{1,0:T(8,128)(2,1)S(1)}, bf16[96,768]{1,0:T(8,128)(2,1)S(1)}, u32[]{:S(2)}, u32[]{:S(2)}) collective-permute-start(bf16[96,768]{1,0:T(8,128)(2,1)S(1)} %get-tuple-element.309), channel_id=1, source_target_pairs={{0,2},{1,3},{2,0},{3,1},{4,6},{5,7},{6,4},{7,5},{8,10},{9,11},{10,... | collective-permute-start | bytes 442376 | tf_op jit(solution)/shard_map/ppermute | solution.py:160
  419.0 12.0 %collective-permute-start.14 = (bf16[96,768]{1,0:T(8,128)(2,1)S(1)}, bf16[96,768]{1,0:T(8,128)(2,1)S(1)}, u32[]{:S(2)}, u32[]{:S(2)}) collective-permute-start(bf16[96,768]{1,0:T(8,128)(2,1)S(1)} %get-tuple-element.308), channel_id=1, source_target_pairs={{0,3},{1,2},{2,1},{3,0},{4,7},{5,6},{6,5},{7,4},{8,11},{9,10},{10,... | collective-permute-start | bytes 442376 | tf_op jit(solution)/shard_map/ppermute | solution.py:160
  430.2 23.3 %collective-permute-start.28 = (bf16[1,4,96,768]{3,2,1,0:T(8,128)(2,1)S(1)}, bf16[1,4,96,768]{3,2,1,0:T(8,128)(2,1)S(1)}, u32[]{:S(2)}, u32[]{:S(2)}) collective-permute-start(bf16[1,4,96,768]{3,2,1,0:T(8,128)(2,1)S(1)} %slice.271), channel_id=1, source_target_pairs={{0,16},{1,17},{2,18},{3,19},{4,12},{5,13},{6,14},{7,15},{8,24},{9,... | collective-permute-start | bytes 1769480 | tf_op jit(solution)/shard_map/ppermute | solution.py:160
  431.1 12.1 %collective-permute-start.15 = (bf16[1,96,768]{2,1,0:T(8,128)(2,1)S(1)}, bf16[1,96,768]{2,1,0:T(8,128)(2,1)S(1)}, u32[]{:S(2)}, u32[]{:S(2)}) collective-permute-start(bf16[1,96,768]{2,1,0:T(8,128)(2,1)S(1)} %fusion.73), channel_id=1, source_target_pairs={{0,16},{1,17},{2,18},{3,19},{4,12},{5,13},{6,14},{7,15},{8,24},{9,... | collective-permute-start | bytes 442376 | tf_op jit(solution)/shard_map/ppermute | solution.py:160
  443.2 10.4 %collective-permute-start.16 = (bf16[2,96,768]{2,1,0:T(8,128)(2,1)S(1)}, bf16[2,96,768]{2,1,0:T(8,128)(2,1)S(1)}, u32[]{:S(2)}, u32[]{:S(2)}) collective-permute-start(bf16[2,96,768]{2,1,0:T(8,128)(2,1)S(1)} %pad_maximum_fusion.6), channel_id=1, source_target_pairs={{0,8},{1,9},{2,10},{3,11},{4,20},{5,21},{6,22},{7,23},{8,0},{9,1},... | collective-permute-start | bytes 884744 | tf_op jit(solution)/shard_map/ppermute | solution.py:160
  447.2 8.7 %collective-permute-start.35 = (bf16[96,768]{1,0:T(8,128)(2,1)S(1)}, bf16[96,768]{1,0:T(8,128)(2,1)S(1)}, u32[]{:S(2)}, u32[]{:S(2)}) collective-permute-start(bf16[96,768]{1,0:T(8,128)(2,1)S(1)} %get-tuple-element.301), channel_id=1, source_target_pairs={{0,1},{1,0},{2,3},{3,2},{4,5},{5,4},{6,7},{7,6},{8,9},{9,8},{10,11... | collective-permute-start | bytes 442376 | tf_op jit(solution)/shard_map/ppermute | solution.py:160
  451.0 9.0 %collective-permute-start.36 = (bf16[96,768]{1,0:T(8,128)(2,1)S(1)}, bf16[96,768]{1,0:T(8,128)(2,1)S(1)}, u32[]{:S(2)}, u32[]{:S(2)}) collective-permute-start(bf16[96,768]{1,0:T(8,128)(2,1)S(1)} %get-tuple-element.303), channel_id=1, source_target_pairs={{0,2},{1,3},{2,0},{3,1},{4,6},{5,7},{6,4},{7,5},{8,10},{9,11},{10,... | collective-permute-start | bytes 442376 | tf_op jit(solution)/shard_map/ppermute | solution.py:160
  451.0 9.0 %collective-permute-start.37 = (bf16[96,768]{1,0:T(8,128)(2,1)S(1)}, bf16[96,768]{1,0:T(8,128)(2,1)S(1)}, u32[]{:S(2)}, u32[]{:S(2)}) collective-permute-start(bf16[96,768]{1,0:T(8,128)(2,1)S(1)} %get-tuple-element.302), channel_id=1, source_target_pairs={{0,3},{1,2},{2,1},{3,0},{4,7},{5,6},{6,5},{7,4},{8,11},{9,10},{10,... | collective-permute-start | bytes 442376 | tf_op jit(solution)/shard_map/ppermute | solution.py:160
  453.7 19.5 %collective-permute-start.17 = (bf16[4,96,768]{2,1,0:T(8,128)(2,1)S(1)}, bf16[4,96,768]{2,1,0:T(8,128)(2,1)S(1)}, u32[]{:S(2)}, u32[]{:S(2)}) collective-permute-start(bf16[4,96,768]{2,1,0:T(8,128)(2,1)S(1)} %pad_maximum_fusion.5), channel_id=1, source_target_pairs={{0,4},{1,5},{2,6},{3,7},{4,0},{5,1},{6,2},{7,3},{8,12},{9,13},{10,... | collective-permute-start | bytes 1769480 | tf_op jit(solution)/shard_map/ppermute | solution.py:160
  453.8 10.4 %collective-permute-start.29 = (bf16[96,768]{1,0:T(8,128)(2,1)S(1)}, bf16[96,768]{1,0:T(8,128)(2,1)S(1)}, u32[]{:S(2)}, u32[]{:S(2)}) collective-permute-start(bf16[96,768]{1,0:T(8,128)(2,1)S(1)} %get-tuple-element.304), channel_id=1, source_target_pairs={{0,1},{1,0},{2,3},{3,2},{4,5},{5,4},{6,7},{7,6},{8,9},{9,8},{10,11... | collective-permute-start | bytes 442376 | tf_op jit(solution)/shard_map/ppermute | solution.py:160
  455.9 16.5 %collective-permute-start.30 = (bf16[96,768]{1,0:T(8,128)(2,1)S(1)}, bf16[96,768]{1,0:T(8,128)(2,1)S(1)}, u32[]{:S(2)}, u32[]{:S(2)}) collective-permute-start(bf16[96,768]{1,0:T(8,128)(2,1)S(1)} %get-tuple-element.306), channel_id=1, source_target_pairs={{0,2},{1,3},{2,0},{3,1},{4,6},{5,7},{6,4},{7,5},{8,10},{9,11},{10,... | collective-permute-start | bytes 442376 | tf_op jit(solution)/shard_map/ppermute | solution.py:160
  460.0 14.1 %copy-start.51 = (pred[8]{0:T(512)(128)(4,1)S(1)}, pred[8]{0:T(512)(128)(4,1)}, u32[]{:S(2)}) copy-start(pred[8]{0:T(512)(128)(4,1)} %get-tuple-element.334) | copy-start | bytes 28
  460.0 12.4 %collective-permute-start.31 = (bf16[96,768]{1,0:T(8,128)(2,1)S(1)}, bf16[96,768]{1,0:T(8,128)(2,1)S(1)}, u32[]{:S(2)}, u32[]{:S(2)}) collective-permute-start(bf16[96,768]{1,0:T(8,128)(2,1)S(1)} %get-tuple-element.305), channel_id=1, source_target_pairs={{0,3},{1,2},{2,1},{3,0},{4,7},{5,6},{6,5},{7,4},{8,11},{9,10},{10,... | collective-permute-start | bytes 442376 | tf_op jit(solution)/shard_map/ppermute | solution.py:160
  474.3 11.9 %collective-permute-start.23 = (bf16[192,768]{1,0:T(8,128)(2,1)S(1)}, bf16[192,768]{1,0:T(8,128)(2,1)S(1)}, u32[]{:S(2)}, u32[]{:S(2)}) collective-permute-start(bf16[192,768]{1,0:T(8,128)(2,1)S(1)} %bitcast.344), channel_id=1, source_target_pairs={{0,1},{1,0},{2,3},{3,2},{4,5},{5,4},{6,7},{7,6},{8,9},{9,8},{10,11... | collective-permute-start | bytes 884744 | tf_op jit(solution)/shard_map/ppermute | solution.py:160
  476.5 23.5 %collective-permute-start.24 = (bf16[192,768]{1,0:T(8,128)(2,1)S(1)}, bf16[192,768]{1,0:T(8,128)(2,1)S(1)}, u32[]{:S(2)}, u32[]{:S(2)}) collective-permute-start(bf16[192,768]{1,0:T(8,128)(2,1)S(1)} %bitcast.345), channel_id=1, source_target_pairs={{0,2},{1,3},{2,0},{3,1},{4,6},{5,7},{6,4},{7,5},{8,10},{9,11},{10,... | collective-permute-start | bytes 884744 | tf_op jit(solution)/shard_map/ppermute | solution.py:160
  476.5 23.5 %collective-permute-start.25 = (bf16[192,768]{1,0:T(8,128)(2,1)S(1)}, bf16[192,768]{1,0:T(8,128)(2,1)S(1)}, u32[]{:S(2)}, u32[]{:S(2)}) collective-permute-start(bf16[192,768]{1,0:T(8,128)(2,1)S(1)} %bitcast.346), channel_id=1, source_target_pairs={{0,3},{1,2},{2,1},{3,0},{4,7},{5,6},{6,5},{7,4},{8,11},{9,10},{10,... | collective-permute-start | bytes 884744 | tf_op jit(solution)/shard_map/ppermute | solution.py:160
  480.5 20.6 %copy-start.46 = (pred[4]{0:T(512)(128)(4,1)S(1)}, pred[4]{0:T(512)(128)(4,1)}, u32[]{:S(2)}) copy-start(pred[4]{0:T(512)(128)(4,1)} %copy-done.44) | copy-start | bytes 16
  (71 other events, 333.6 us)
